TPU v7x, 256 devices: a whole 4x4x8 slice. The times are simulated.
256 devices in a mesh: section: 2 (over core), fsdp: 2 (over z_lo), tok: 64 (over x, z_hi, y).
Axes of the slice: x: 4, y: 4, z: 8 (z_hi: 4, z_lo: 2; z = z_hi * 2 + z_lo), core: 2. Of those that a mesh axis runs over, the one named last changes fastest.
Arguments:
- hidden: bfloat16 [4, 256, 3072], P(None, 'tok'), may hold values from -6 to 6
- lengths: int32 [4], replicated, may hold values from 1 to 256, 768 in all
- text_count: int32 [1], replicated, may hold values from 1 to 256
- timestep: int32 [1], replicated, may hold values from 0 to 49
- mod_table: bfloat16 [2, 50, 6, 3072], P('section'), may hold values from -3 to 3
- w_qkv: bfloat16 [2, 3072, 3, 1536], P('section', 'tok', None, 'fsdp'), may hold values from -0.109375 to 0.109375
- w_out: bfloat16 [2, 3072, 1536], P('section', 'tok', 'fsdp'), may hold values from -0.15625 to 0.15625
- qk_gain: float32 [2, 2, 64], P('section'), may hold values from 0.5 to 2
- stale_cache: bfloat16 [2, 2, 4, 256, 1536], P('section', None, None, None, 'fsdp'), may hold values from -6 to 6
Outputs:
- layer_out: bfloat16 [2, 4, 256, 3072], P('section', None, 'tok')
- new_cache: bfloat16 [2, 2, 4, 256, 1536], P('section', None, None, None, 'fsdp')
Inputs may be any that keep to these rules, and one draw needn't show every extreme that they name: The lengths sum to 768; one patch is full with exactly 256 live tokens.
All inputs are finite; a program needn't handle non-finite values.
Results may differ from a plain program's by a relative error of at most 0.012.
Values may be sent and summed in bfloat16 or wider, within the bound.
A program may use at most 128 MiB of HBM per device.

v0:
```python
import jax
import jax.numpy as jnp
from jax import lax
from jax.sharding import PartitionSpec as P

HEAD_DIM = 64


def from_behind(block, axis, distance):
    devices = range(lax.axis_size(axis))
    route = [(i - distance, i) for i in devices if i - distance in devices]
    return lax.ppermute(block, axis, route)


def layer_norm(values, eps):
    mean = jnp.mean(values, axis=-1, keepdims=True)
    centred = values - mean
    spread = jnp.mean(centred * centred, axis=-1, keepdims=True)
    return centred * lax.rsqrt(spread + eps)


def modulate(inputs, positions, modulation, text_total):
    is_text = (positions < text_total)[:, None]
    shift = jnp.where(is_text, modulation[3], modulation[0])
    scale = jnp.where(is_text, modulation[4], modulation[1])
    gate = jnp.where(is_text, modulation[5], modulation[2])
    normed = layer_norm(inputs, 1e-05)
    return ((normed * (1.0 + scale) + shift).astype(jnp.bfloat16), gate)


def project_heads(mixed, gains):
    queries = (layer_norm(mixed[:, 0], 1e-06) * gains[0]).astype(jnp.bfloat16)
    keys_new = (layer_norm(mixed[:, 1], 1e-06) * gains[1]).astype(jnp.bfloat16)
    values_new = mixed[:, 2].astype(jnp.bfloat16)
    return (queries, keys_new, values_new)


def attend(queries, keys_all, values_all, key_live):
    scores = jnp.einsum(
        "qhd,khd->hqk", queries, keys_all, preferred_element_type=jnp.float32
    ) * HEAD_DIM ** (-0.5)
    scores = jnp.where(key_live[None, None, :], scores, -jnp.inf)
    top = jnp.max(scores, axis=-1, keepdims=True)
    expo = jnp.exp(scores - top)
    weights = (expo / jnp.sum(expo, axis=-1, keepdims=True)).astype(jnp.bfloat16)
    return jnp.einsum(
        "hqk,khd->qhd", weights, values_all, preferred_element_type=jnp.float32
    ).astype(jnp.bfloat16)


def local(hidden, lengths, text_count, timestep, mod_table, w_qkv, w_out, qk_gain, stale_cache):
    section_index = lax.axis_index("section")
    section_count = lax.axis_size("section")
    tok_index = lax.axis_index("tok")
    tok_count = lax.axis_size("tok")
    patches, cap_dev, width = hidden.shape
    cap_all = cap_dev * tok_count
    local_width = w_qkv.shape[3]
    heads_local = local_width // HEAD_DIM
    rows_local = jnp.arange(cap_dev, dtype=jnp.int32) + tok_index * cap_dev
    key_rows = jnp.arange(cap_all, dtype=jnp.int32)
    key_live = (key_rows[None, :] < lengths[:, None]).reshape(-1)
    offsets = jnp.cumsum(lengths) - lengths
    modulation = lax.dynamic_index_in_dim(mod_table[0], timestep[0], 0, keepdims=False).astype(
        jnp.float32
    )
    gains = qk_gain[0]
    shard_in = w_qkv[0].reshape(w_qkv.shape[1], 3 * local_width)
    out_local = w_out[0]
    weight_in, weight_out = (
        lax.all_gather(shard_in, "tok", axis=0, tiled=True),
        lax.all_gather(out_local, "tok", axis=0, tiled=True),
    )
    cache_keys = stale_cache[0, 0]
    cache_values = stale_cache[0, 1]
    out_states = jnp.zeros((patches, cap_dev, width), jnp.bfloat16)
    incoming = jnp.zeros((cap_dev, width), jnp.bfloat16)
    ticks = patches + section_count - 1
    for tick in range(ticks):
        patch = tick - section_index
        is_live = (patch >= 0) & (patch < patches)
        patch_slot = jnp.clip(patch, 0, patches - 1)
        own_states = hidden[min(tick, patches - 1)]
        inputs = jnp.where(section_index == 0, own_states, incoming).astype(jnp.float32)
        row_live = rows_local < lengths[patch_slot]
        modded, gate = modulate(inputs, offsets[patch_slot] + rows_local, modulation, text_count[0])
        mixed = jnp.dot(modded, weight_in, preferred_element_type=jnp.float32)
        mixed = mixed.reshape(cap_dev, 3, heads_local, HEAD_DIM)
        queries, keys_new, values_new = project_heads(mixed, gains)
        keys_new = jnp.where(row_live[:, None, None], keys_new, jnp.zeros_like(keys_new)).reshape(
            cap_dev, local_width
        )
        values_new = jnp.where(
            row_live[:, None, None], values_new, jnp.zeros_like(values_new)
        ).reshape(cap_dev, local_width)
        fresh_keys, fresh_values = (
            lax.all_gather(keys_new, "tok", axis=0, tiled=True),
            lax.all_gather(values_new, "tok", axis=0, tiled=True),
        )
        cache_keys = jnp.where(
            is_live,
            lax.dynamic_update_index_in_dim(cache_keys, fresh_keys, patch_slot, 0),
            cache_keys,
        )
        cache_values = jnp.where(
            is_live,
            lax.dynamic_update_index_in_dim(cache_values, fresh_values, patch_slot, 0),
            cache_values,
        )
        attended = attend(
            queries,
            cache_keys.reshape(-1, heads_local, HEAD_DIM),
            cache_values.reshape(-1, heads_local, HEAD_DIM),
            key_live,
        ).reshape(cap_dev, local_width)
        partial_out = lax.dot_general(
            attended, weight_out, (((1,), (1,)), ((), ())), preferred_element_type=jnp.float32
        )
        projected = lax.psum(partial_out.astype(jnp.bfloat16), "fsdp").astype(jnp.float32)
        result = jnp.where(row_live[:, None], inputs + gate * projected, 0.0).astype(jnp.bfloat16)
        out_states = jnp.where(
            is_live, lax.dynamic_update_index_in_dim(out_states, result, patch_slot, 0), out_states
        )
        if tick + 1 < ticks:
            incoming = from_behind(result, "section", 1)
    return (out_states[None], jnp.stack([cache_keys, cache_values])[None])


def solution(mesh):
    in_specs = (
        P(None, "tok", None),
        P(),
        P(),
        P(),
        P("section", None, None, None),
        P("section", "tok", None, "fsdp"),
        P("section", "tok", "fsdp"),
        P("section", None, None),
        P("section", None, None, None, "fsdp"),
    )
    out_specs = (P("section", None, "tok", None), P("section", None, None, None, "fsdp"))
    return jax.shard_map(local, mesh=mesh, in_specs=in_specs, out_specs=out_specs, check_vma=False)
```

profile of v0, /device:TPU:40, one launch (start us, length us, event | category | flops | bytes accessed | tf_op | source)
XLA Modules:
  0.0 2399.3 jit_solution(7647845240221618332)
XLA Ops:
  25.0 4.4 fusion.206
  29.4 135.6 %all-gather.14.cloned.1.call-done = bf16[3072,2304]{1,0:T(8,128)(2,1)} async-done(((bf16[48,2304]{1,0:T(8,128)(2,1)}), bf16[3072,2304]{1,0:T(8,128)(2,1)}) %all-gather.14.cloned.1.call-update) | async-done | bytes 14155792 | tf_op jit(solution)/shard_map/all_gather | solution.py:71
  165.1 18.7 copy.136
  183.8 9.0 fusion.116
  194.0 198.5 %all-gather.1 = bf16[64,4,768]{2,1,0:T(4,128)(2,1)} all-gather(bf16[1,4,768]{2,1,0:T(4,128)(2,1)S(1)} %get-tuple-element.70), channel_id=1, replica_groups=mesh['section'=2,'fsdp'=2,'tok'=64] {'tok'}, dimensions={0}, use_global_device_ids=true | all-gather | bytes 399360 | tf_op jit(solution)/shard_map/all_gather | solution.py:98
  394.3 201.3 %all-gather.2 = bf16[64,4,768]{2,1,0:T(4,128)(2,1)} all-gather(bf16[1,4,768]{2,1,0:T(4,128)(2,1)S(1)} %get-tuple-element.69), channel_id=1, replica_groups=mesh['section'=2,'fsdp'=2,'tok'=64] {'tok'}, dimensions={0}, use_global_device_ids=true | all-gather | bytes 399360 | tf_op jit(solution)/shard_map/all_gather | solution.py:97
  599.0 2.2 copy.148
  601.2 3.8 reshape.581
  605.0 2.2 copy.138
  607.2 3.8 reshape.580
  616.0 3.7 fusion.15
  619.6 9.4 psum.35
  631.7 7.6 fusion.105
  649.1 195.5 %all-gather.4 = bf16[64,4,768]{2,1,0:T(4,128)(2,1)} all-gather(bf16[1,4,768]{2,1,0:T(4,128)(2,1)S(1)} %get-tuple-element.67), channel_id=1, replica_groups=mesh['section'=2,'fsdp'=2,'tok'=64] {'tok'}, dimensions={0}, use_global_device_ids=true | all-gather | bytes 399360 | tf_op jit(solution)/shard_map/all_gather | solution.py:97
  847.6 2.2 copy.156
  849.8 3.8 reshape.585
  856.3 197.8 %all-gather.3 = bf16[64,4,768]{2,1,0:T(4,128)(2,1)} all-gather(bf16[1,4,768]{2,1,0:T(4,128)(2,1)S(1)} %get-tuple-element.68), channel_id=1, replica_groups=mesh['section'=2,'fsdp'=2,'tok'=64] {'tok'}, dimensions={0}, use_global_device_ids=true | all-gather | bytes 399360 | tf_op jit(solution)/shard_map/all_gather | solution.py:98
  1057.0 2.2 copy.150
  1059.2 3.8 reshape.584
  1065.3 3.7 fusion.18
  1068.9 6.9 psum.36
  1078.4 7.6 fusion.107
  1095.8 195.7 %all-gather.6 = bf16[64,4,768]{2,1,0:T(4,128)(2,1)} all-gather(bf16[1,4,768]{2,1,0:T(4,128)(2,1)S(1)} %get-tuple-element.65), channel_id=1, replica_groups=mesh['section'=2,'fsdp'=2,'tok'=64] {'tok'}, dimensions={0}, use_global_device_ids=true | all-gather | bytes 399360 | tf_op jit(solution)/shard_map/all_gather | solution.py:97
  1294.5 2.2 copy.164
  1296.7 3.8 reshape.589
  1303.3 197.4 %all-gather.5 = bf16[64,4,768]{2,1,0:T(4,128)(2,1)} all-gather(bf16[1,4,768]{2,1,0:T(4,128)(2,1)S(1)} %get-tuple-element.66), channel_id=1, replica_groups=mesh['section'=2,'fsdp'=2,'tok'=64] {'tok'}, dimensions={0}, use_global_device_ids=true | all-gather | bytes 399360 | tf_op jit(solution)/shard_map/all_gather | solution.py:98
  1503.6 2.2 copy.158
  1505.8 3.8 reshape.588
  1511.9 3.7 fusion.21
  1515.5 8.7 psum.37
  1526.9 7.6 fusion.109
  1544.3 195.8 %all-gather.8 = bf16[64,4,768]{2,1,0:T(4,128)(2,1)} all-gather(bf16[1,4,768]{2,1,0:T(4,128)(2,1)S(1)} %get-tuple-element.63), channel_id=1, replica_groups=mesh['section'=2,'fsdp'=2,'tok'=64] {'tok'}, dimensions={0}, use_global_device_ids=true | all-gather | bytes 399360 | tf_op jit(solution)/shard_map/all_gather | solution.py:97
  1743.1 2.2 copy.172
  1745.3 3.8 reshape.593
  1751.8 197.5 %all-gather.7 = bf16[64,4,768]{2,1,0:T(4,128)(2,1)} all-gather(bf16[1,4,768]{2,1,0:T(4,128)(2,1)S(1)} %get-tuple-element.64), channel_id=1, replica_groups=mesh['section'=2,'fsdp'=2,'tok'=64] {'tok'}, dimensions={0}, use_global_device_ids=true | all-gather | bytes 399360 | tf_op jit(solution)/shard_map/all_gather | solution.py:98
  1952.3 2.2 copy.166
  1954.5 3.8 reshape.592
  1960.5 3.7 fusion.24
  1964.2 6.9 psum.38
  1974.5 7.0 fusion.111
  1984.1 185.9 %all-gather.10 = bf16[64,4,768]{2,1,0:T(4,128)(2,1)S(1)} all-gather(bf16[1,4,768]{2,1,0:T(4,128)(2,1)S(1)} %get-tuple-element.51), channel_id=1, replica_groups=mesh['section'=2,'fsdp'=2,'tok'=64] {'tok'}, dimensions={0}, use_global_device_ids=true | all-gather | bytes 399360 | tf_op jit(solution)/shard_map/all_gather | solution.py:97
  2170.8 187.8 %all-gather.9 = bf16[64,4,768]{2,1,0:T(4,128)(2,1)S(1)} all-gather(bf16[1,4,768]{2,1,0:T(4,128)(2,1)} %get-tuple-element.52), channel_id=1, replica_groups=mesh['section'=2,'fsdp'=2,'tok'=64] {'tok'}, dimensions={0}, use_global_device_ids=true | all-gather | bytes 399360 | tf_op jit(solution)/shard_map/all_gather | solution.py:98
  2360.4 2.2 copy.180
  2362.6 3.8 reshape.597
  2368.4 2.2 copy.174
  2370.6 3.8 reshape.596
  2376.5 3.7 fusion.27
  2380.2 8.8 psum.39
  (273 shorter events, 113.3 us)
Async XLA Ops:
  7.2 157.9 %all-gather.14.cloned.1.call-start = ((), (), s32[]{:S(2)}) async-start(), calls=%async_computation | async-start | bytes 14376960 | tf_op jit(solution)/shard_map/all_gather | solution.py:71
  9.0 606.9 %all-gather.16.cloned.1.call-start = ((), (), s32[]{:S(2)}) async-start(), calls=%async_computation.1 | async-start | bytes 4792320 | tf_op jit(solution)/shard_map/all_gather | solution.py:72
  12.7 598.3 %copy-start.20 = (f32[64]{0:T(128)}, f32[64]{0:T(128)S(1)}, u32[]{:S(2)}) copy-start(f32[64]{0:T(128)S(1)} %get-tuple-element.49) | copy-start | bytes 772
  29.4 1941.7 %copy-start.3 = (f32[1,1,1,3072]{3,1,2,0:T(1,128)}, f32[1,1,1,3072]{3,1,2,0:T(1,128)S(1)}, u32[]{:S(2)}) copy-start(f32[1,1,1,3072]{3,1,2,0:T(1,128)S(1)} %get-tuple-element.47) | copy-start | bytes 36868
  165.1 18.7 copy-start.5
  612.8 0.7 copy-start.13
  629.2 2.1 collective-permute-start
  631.2 8.2 copy-start.28
  645.3 0.5 copy-start.17
  849.8 3.8 copy-start.7
  849.8 3.8 copy-start.14
  849.8 3.8 copy-start.21
  855.4 0.7 copy-start.10
  1065.3 10.6 copy-start.29
  1065.3 10.6 copy-start.38
  1075.9 2.1 collective-permute-start.1
  1077.8 8.2 copy-start.30
  1092.0 0.5 copy-start.18
  1296.7 3.8 copy-start.8
  1296.7 3.8 copy-start.15
  1296.7 3.8 copy-start.22
  1302.3 0.7 copy-start.11
  1511.9 12.4 copy-start.31
  1511.9 12.4 copy-start.37
  1524.4 2.1 collective-permute-start.2
  1526.3 8.2 copy-start.32
  1540.5 0.5 copy-start.19
  1745.3 3.8 copy-start.9
  1745.3 3.8 copy-start.16
  1745.3 3.8 copy-start.23
  1750.9 0.7 copy-start.12
  1960.5 10.6 copy-start.33
  1960.5 10.6 copy-start.36
  1971.2 10.3 copy-start
  1971.2 2.5 collective-permute-start.3
  1973.1 8.4 copy-start.26
  1973.9 0.6 copy-start.1
  1974.5 8.9 copy-start.34
  2359.4 0.6 copy-start.25
  2359.4 0.8 copy-start.6
  2362.6 3.8 copy-start.24
  2389.0 2.0 copy-start.2
  2389.0 2.0 copy-start.4
  2389.0 2.0 copy-start.27
  2389.0 2.0 copy-start.35
Sparse Core Ops, SparseCore 0:
  11.2 153.8 all-gather.13
  168.3 87.9 all-gather.15
where the time goes:
time: 2400 us
  blocking collectives  1990 us (83%)
  waiting for transfers between devices  137 us (6%)
  local copies, waits for them, and re-layouts  126 us (5%)
  matrix products  76.5 us (3%)
  other arithmetic  44.9 us (2%)
    all_gather x5, blocking collectives, local(): lax.all_gather(values_new, 'tok', axis=0, tiled=True)  979 us
    all_gather x5, blocking collectives, local(): lax.all_gather(keys_new, 'tok', axis=0, tiled=True)  974 us
    all_gather x1, waiting for transfers between devices, local(): lax.all_gather(shard_in, 'tok', axis=0, tiled=True)  136 us
  transfers between devices with their start and end apart: 6, of which 4 were waited for; matrix products, arithmetic and copies ran while one was open for 3% of the time, Pallas kernels for 0%

commit v1 on v0

--- a/solution.py
+++ b/solution.py
@@ -94,7 +94,9 @@
             row_live[:, None, None], values_new, jnp.zeros_like(values_new)
         ).reshape(cap_dev, local_width)
         fresh_keys, fresh_values = (
-            lax.all_gather(keys_new, "tok", axis=0, tiled=True),
+            jnp.concatenate(
+                lax.all_to_all(jnp.stack([keys_new] * lax.axis_size("tok")), "tok", 0, 0), axis=0
+            ),
             lax.all_gather(values_new, "tok", axis=0, tiled=True),
         )
         cache_keys = jnp.where(

time: 2400 us -> 1520 us (0.63)
  blocking collectives: 1990 us -> 1050 us
  starting transfers between devices: 5.23 us -> 41.7 us
    all_gather x5 -> x0, blocking collectives: 974 us -> none  [local(): lax.all_gather(keys_new, 'tok', axis=0, tiled=True)]
    all_to_all x0 -> x5, starting transfers between devices: none -> 36.3 us  [local(): lax.all_to_all(jnp.stack([keys_new] * lax.axis_size('tok')), 'tok', 0, 0)]
  transfers between devices with their start and end apart: 6 -> 11, of which waited for: 4 -> 3; matrix products, arithmetic and copies ran while one was open for 3% -> 7% of each run, Pallas kernels for 0% -> 0%
where the time goes in v1:
time: 1520 us; the launch traced here: 1510 us
  blocking collectives  1050 us (69%)
  waiting for transfers between devices  143 us (9%)
  local copies, waits for them, and re-layouts  132 us (9%)
  matrix products  76.5 us (5%)
  other arithmetic  44.3 us (3%)
  starting transfers between devices  41.7 us (3%)
  between operations  16.2 us (1%)
    all_gather x5, blocking collectives, local(): lax.all_gather(values_new, 'tok', axis=0, tiled=True)  999 us
    all_gather x1, waiting for transfers between devices, local(): lax.all_gather(shard_in, 'tok', axis=0, tiled=True)  142 us
    psum x5, blocking collectives, local(): lax.psum(partial_out.astype(jnp.bfloat16), 'fsdp').astype(jnp.float32)  55.5 us
    dot_general x5, matrix products, local(): mixed = jnp.dot(modded, weight_in, preferred_element_type=jnp.float32)  38.8 us
    all_to_all x5, starting transfers between devices, local(): lax.all_to_all(jnp.stack([keys_new] * lax.axis_size('tok')), 'tok', 0, 0)  36.3 us
  transfers between devices with their start and end apart: 11, of which 3 were waited for; matrix products, arithmetic and copies ran while one was open for 7% of the time, Pallas kernels for 0%

profile of v1, /device:TPU:40, one launch (start us, length us, event | category | flops | bytes accessed | tf_op | source)
XLA Modules:
  0.0 1507.8 jit_solution(9527867642749937323)
XLA Ops:
  24.0 141.7 %all-gather.9.cloned.1.call-done = bf16[3072,2304]{1,0:T(8,128)(2,1)} async-done(((bf16[48,2304]{1,0:T(8,128)(2,1)}), bf16[3072,2304]{1,0:T(8,128)(2,1)}) %all-gather.9.cloned.1.call-update) | async-done | bytes 14155792 | tf_op jit(solution)/shard_map/all_gather | solution.py:71
  165.7 18.7 %copy.136 = bf16[2304,3072]{1,0:T(8,128)(2,1)} copy(bf16[2304,3072]{0,1:T(8,128)(2,1)} %bitcast.280) | data formatting | bytes 28311552 | tf_op jit(solution)/shard_map/dot_general | solution.py:87
  184.4 9.0 fusion.117
  195.4 9.9 all-to-all-start
  206.5 4.3 fusion.202
  210.9 198.8 %all-gather.1 = bf16[64,4,768]{2,1,0:T(4,128)(2,1)} all-gather(bf16[1,4,768]{2,1,0:T(4,128)(2,1)S(1)} %get-tuple-element.70), channel_id=1, replica_groups=mesh['section'=2,'fsdp'=2,'tok'=64] {'tok'}, dimensions={0}, use_global_device_ids=true | all-gather | bytes 399360 | tf_op jit(solution)/shard_map/all_gather | solution.py:100
  415.0 2.2 copy.148
  417.2 3.8 reshape.624
  421.0 2.2 copy.138
  423.1 3.8 reshape.623
  431.9 3.7 fusion.15
  435.5 13.8 psum.35
  451.9 7.6 fusion.106
  469.0 6.7 all-to-all-start.1
  475.7 202.4 %all-gather.2 = bf16[64,4,768]{2,1,0:T(4,128)(2,1)} all-gather(bf16[1,4,768]{2,1,0:T(4,128)(2,1)S(1)} %get-tuple-element.68), channel_id=1, replica_groups=mesh['section'=2,'fsdp'=2,'tok'=64] {'tok'}, dimensions={0}, use_global_device_ids=true | all-gather | bytes 399360 | tf_op jit(solution)/shard_map/all_gather | solution.py:100
  681.0 2.2 copy.150
  683.3 3.8 reshape.627
  690.2 2.2 copy.156
  692.4 3.8 reshape.628
  701.1 3.7 fusion.18
  704.8 6.8 psum.36
  714.3 7.6 fusion.108
  731.3 7.3 all-to-all-start.2
  738.6 197.2 %all-gather.3 = bf16[64,4,768]{2,1,0:T(4,128)(2,1)} all-gather(bf16[1,4,768]{2,1,0:T(4,128)(2,1)S(1)} %get-tuple-element.66), channel_id=1, replica_groups=mesh['section'=2,'fsdp'=2,'tok'=64] {'tok'}, dimensions={0}, use_global_device_ids=true | all-gather | bytes 399360 | tf_op jit(solution)/shard_map/all_gather | solution.py:100
  938.8 2.2 copy.158
  941.0 3.8 reshape.631
  948.0 2.2 copy.164
  950.2 3.8 reshape.632
  958.9 3.7 fusion.21
  962.5 14.3 psum.37
  979.5 7.6 fusion.110
  996.6 6.3 all-to-all-start.3
  1002.9 202.7 %all-gather.4 = bf16[64,4,768]{2,1,0:T(4,128)(2,1)} all-gather(bf16[1,4,768]{2,1,0:T(4,128)(2,1)S(1)} %get-tuple-element.64), channel_id=1, replica_groups=mesh['section'=2,'fsdp'=2,'tok'=64] {'tok'}, dimensions={0}, use_global_device_ids=true | all-gather | bytes 399360 | tf_op jit(solution)/shard_map/all_gather | solution.py:100
  1208.5 2.2 copy.166
  1210.7 3.8 reshape.635
  1217.7 2.2 copy.172
  1219.9 3.8 reshape.636
  1228.6 3.7 fusion.24
  1232.3 6.8 psum.38
  1242.6 7.0 fusion.112
  1253.1 6.1 all-to-all-start.4
  1259.2 197.5 %all-gather.5 = bf16[64,4,768]{2,1,0:T(4,128)(2,1)} all-gather(bf16[1,4,768]{2,1,0:T(4,128)(2,1)} %get-tuple-element.52), channel_id=1, replica_groups=mesh['section'=2,'fsdp'=2,'tok'=64] {'tok'}, dimensions={0}, use_global_device_ids=true | all-gather | bytes 399360 | tf_op jit(solution)/shard_map/all_gather | solution.py:100
  1461.2 2.2 copy.174
  1463.4 3.8 reshape.639
  1469.7 2.2 copy.180
  1472.0 3.8 reshape.640
  1479.9 3.7 fusion.27
  1483.6 13.7 psum.39
  (279 shorter events, 119.4 us)
Async XLA Ops:
  7.2 158.5 %all-gather.9.cloned.1.call-start = ((), (), s32[]{:S(2)}) async-start(), calls=%async_computation.5 | async-start | bytes 14376960 | tf_op jit(solution)/shard_map/all_gather | solution.py:71
  9.0 422.8 %all-gather.11.cloned.1.call-start = ((), (), s32[]{:S(2)}) async-start(), calls=%async_computation.6 | async-start | bytes 4792320 | tf_op jit(solution)/shard_map/all_gather | solution.py:72
  12.7 414.3 %copy-start.19 = (f32[64]{0:T(128)}, f32[64]{0:T(128)S(1)}, u32[]{:S(2)}) copy-start(f32[64]{0:T(128)S(1)} %get-tuple-element.49) | copy-start | bytes 772
  24.0 1215.2 %copy-start.3 = (f32[1,1,1,3072]{3,1,2,0:T(1,128)}, f32[1,1,1,3072]{3,1,2,0:T(1,128)S(1)}, u32[]{:S(2)}) copy-start(f32[1,1,1,3072]{3,1,2,0:T(1,128)S(1)} %get-tuple-element.47) | copy-start | bytes 36868
  165.7 18.7 %copy-start.5 = (bf16[4,4,3072]{2,1,0:T(4,128)(2,1)S(1)}, bf16[4,4,3072]{2,1,0:T(4,128)(2,1)}, u32[]{:S(2)}) copy-start(bf16[4,4,3072]{2,1,0:T(4,128)(2,1)} %param.9) | copy-start | bytes 294916
  195.4 216.1 %all-to-all-start = ((bf16[64,4,768]{2,1,0:T(4,128)(2,1)}), bf16[64,4,768]{2,1,0:T(4,128)(2,1)}, u32[]{:S(2)}, u32[]{:S(2)}) async-start(bf16[64,4,768]{2,1,0:T(4,128)(2,1)} %stack.24), calls=%async_computation | async-start | bytes 786432 | tf_op jit(solution)/shard_map/all_to_all | solution.py:98
  428.7 0.7 copy-start.10
  449.4 2.1 collective-permute-start
  451.4 8.2 copy-start.26
  464.2 0.6 copy-start.16
  469.0 218.2 %all-to-all-start.1 = ((bf16[64,4,768]{2,1,0:T(4,128)(2,1)}), bf16[64,4,768]{2,1,0:T(4,128)(2,1)}, u32[]{:S(2)}, u32[]{:S(2)}) async-start(bf16[64,4,768]{2,1,0:T(4,128)(2,1)} %stack.25), calls=%async_computation.1 | async-start | bytes 786432 | tf_op jit(solution)/shard_map/all_to_all | solution.py:98
  683.3 3.8 copy-start.7
  692.4 3.8 copy-start.20
  698.0 0.7 copy-start.11
  701.1 10.5 copy-start.27
  701.1 10.5 copy-start.36
  711.8 2.1 collective-permute-start.1
  713.7 8.2 copy-start.28
  726.6 0.6 copy-start.17
  731.3 213.7 %all-to-all-start.2 = ((bf16[64,4,768]{2,1,0:T(4,128)(2,1)}), bf16[64,4,768]{2,1,0:T(4,128)(2,1)}, u32[]{:S(2)}, u32[]{:S(2)}) async-start(bf16[64,4,768]{2,1,0:T(4,128)(2,1)} %stack.26), calls=%async_computation.2 | async-start | bytes 786432 | tf_op jit(solution)/shard_map/all_to_all | solution.py:98
  941.0 3.8 copy-start.8
  950.2 3.8 copy-start.21
  955.7 0.7 copy-start.12
  958.9 18.0 %copy-start.29 = (pred[4]{0:T(512)(128)(4,1)S(1)}, pred[4]{0:T(512)(128)(4,1)}, u32[]{:S(2)}) copy-start(pred[4]{0:T(512)(128)(4,1)} %copy-done.28) | copy-start | bytes 16
  958.9 18.0 %copy-start.35 = (pred[4]{0:T(512)(128)(4,1)S(1)}, pred[4]{0:T(512)(128)(4,1)}, u32[]{:S(2)}) copy-start(pred[4]{0:T(512)(128)(4,1)} %fusion.190) | copy-start | bytes 16
  977.0 2.1 collective-permute-start.2
  979.1 8.0 copy-start.30
  991.8 0.6 copy-start.18
  996.6 218.2 %all-to-all-start.3 = ((bf16[64,4,768]{2,1,0:T(4,128)(2,1)}), bf16[64,4,768]{2,1,0:T(4,128)(2,1)}, u32[]{:S(2)}, u32[]{:S(2)}) async-start(bf16[64,4,768]{2,1,0:T(4,128)(2,1)} %stack.27), calls=%async_computation.3 | async-start | bytes 786432 | tf_op jit(solution)/shard_map/all_to_all | solution.py:98
  1210.7 3.8 copy-start.9
  1219.9 3.8 copy-start.22
  1225.5 0.7 copy-start.13
  1228.6 10.5 copy-start.31
  1228.6 10.5 copy-start.34
  1239.3 10.3 copy-start
  1239.3 2.6 collective-permute-start.3
  1241.2 8.4 copy-start.24
  1242.0 0.6 copy-start.1
  1242.6 9.0 copy-start.32
  1253.1 215.7 %all-to-all-start.4 = ((bf16[64,4,768]{2,1,0:T(4,128)(2,1)}), bf16[64,4,768]{2,1,0:T(4,128)(2,1)S(1)}, u32[]{:S(2)}, u32[]{:S(2)}) async-start(bf16[64,4,768]{2,1,0:T(4,128)(2,1)} %stack.28), calls=%async_computation.4 | async-start | bytes 786432 | tf_op jit(solution)/shard_map/all_to_all | solution.py:98
  1471.9 3.9 copy-start.6
  1471.9 3.9 copy-start.14
  1472.0 3.9 copy-start.15
  1472.0 3.9 copy-start.23
  1497.3 2.0 copy-start.2
  1497.3 2.0 copy-start.4
  1497.3 2.0 copy-start.25
  1497.3 2.0 copy-start.33
Sparse Core Ops, SparseCore 0:
  11.8 153.8 all-gather.8
  168.9 92.4 all-gather.10
